TPU v7x, 512 devices: a whole 4x4x16 slice. The times are simulated.
512 devices in a mesh: dp: 32 (over y, z_lo), tensor: 16 (over z_hi, x, core).
Axes of the slice: x: 4, y: 4, z: 16 (z_hi: 2, z_lo: 8; z = z_hi * 8 + z_lo), core: 2. Of those that a mesh axis runs over, the one named last changes fastest.
Arguments:
- tokens: bfloat16 [32768, 4608], P(('dp', 'tensor')), may hold values from -24 to 24
- gain: float32 [4608], replicated, may hold values from 0.1 to 1.9
- qk_weight: bfloat16 [4608, 2, 2048], P('dp', None, 'tensor'), may hold values from -0.54506148 to 0.54506148
- value_rows: bfloat16 [32768, 2048], P(('dp', 'tensor')), may hold values from -6 to 6
- context_grad: bfloat16 [32768, 2048], P(('dp', 'tensor')), may hold values from -6 to 6
- first_key: int32 [32768], P('dp'), may hold values from 0 to 32767, as said below
Outputs:
- qkv_grad: bfloat16 [4608, 3, 2048], P('dp', None, 'tensor')
Inputs may be any that keep to these rules, and one draw needn't show every extreme that they name: first_key[i] is the larger of the first position of token i's document and i - 4095; documents stay inside their sequence of 1024 tokens, the last token of each sequence is a document of its own, and first_key[i] <= i.
All inputs are finite; a program needn't handle non-finite values.
Results may differ from a plain program's by a relative error of at most 0.03.
The roundings to bfloat16 on the way count: a program that leaves them out, or rounds other values in their place, can miss the bound.
Values may be sent and summed in bfloat16 or wider, within the bound.
A program may use at most 64 MiB of HBM per device.

v0:
```python
import jax
import jax.numpy as jnp
from jax import lax
from jax.sharding import PartitionSpec as P

HD = 128


epsilon = 1e-06
softcap = 50.0
query_scale = 144.0 ** (-0.5)


def local(tokens, gain, qk_weight, value_rows, context_grad, first_key):
    width = tokens.shape[1]
    shard_rows = qk_weight.shape[0]
    head_cols = qk_weight.shape[2]
    head_count = head_cols // HD
    floated = tokens.astype(jnp.float32)
    mean_sq = jnp.mean(floated * floated, axis=1, keepdims=True)
    normed = (floated * lax.rsqrt(mean_sq + epsilon) * gain).astype(jnp.bfloat16)
    normed_all = lax.all_gather(normed, "tensor", axis=0, tiled=True)
    seq_len = normed_all.shape[0]
    whole_w = lax.all_gather(qk_weight, "dp", axis=0, tiled=True).reshape(width, 2 * head_cols)
    projected = jnp.dot(normed_all, whole_w, preferred_element_type=jnp.float32).astype(
        jnp.bfloat16
    )
    queries = projected[:, :head_cols].reshape(seq_len, head_count, HD)
    keys_all = projected[:, head_cols:].reshape(seq_len, head_count, HD)
    cot_flat, value_flat_in = (
        lax.all_to_all(context_grad, "tensor", split_axis=1, concat_axis=0, tiled=True),
        lax.all_to_all(value_rows, "tensor", split_axis=1, concat_axis=0, tiled=True),
    )
    cotangent = cot_flat.reshape(seq_len, head_count, HD)
    values_all = value_flat_in.reshape(seq_len, head_count, HD)
    positions = lax.axis_index("dp") * seq_len + jnp.arange(seq_len, dtype=jnp.int32)
    block = min(512, seq_len)
    value_acc = jnp.zeros((seq_len, head_count, HD), jnp.float32)
    key_acc = jnp.zeros((seq_len, head_count, HD), jnp.float32)
    query_parts = []
    for blk_index in range(seq_len // block):
        lo = blk_index * block
        query_blk = queries[lo : lo + block]
        cot_blk = cotangent[lo : lo + block]
        pos_blk = positions[lo : lo + block]
        start_blk = first_key[lo : lo + block]
        raw = (
            jnp.einsum("qhd,khd->hqk", query_blk, keys_all, preferred_element_type=jnp.float32)
            * query_scale
        )
        tanh_val = jnp.tanh(raw / softcap)
        capped = softcap * tanh_val
        seen = (positions[None, :] >= start_blk[:, None]) & (positions[None, :] <= pos_blk[:, None])
        raised = jnp.where(seen[None], jnp.exp(capped), 0.0)
        probs = raised / jnp.sum(raised, axis=2, keepdims=True)
        probs_low = probs.astype(jnp.bfloat16)
        value_acc = value_acc + jnp.einsum(
            "hqk,qhd->khd", probs_low, cot_blk, preferred_element_type=jnp.float32
        )
        dprobs = jnp.einsum("qhd,khd->hqk", cot_blk, values_all, preferred_element_type=jnp.float32)
        inner = jnp.sum(probs * dprobs, axis=2, keepdims=True)
        dscore = (probs * (dprobs - inner) * (1.0 - tanh_val * tanh_val) * query_scale).astype(
            jnp.bfloat16
        )
        query_parts.append(
            jnp.einsum("hqk,khd->qhd", dscore, keys_all, preferred_element_type=jnp.float32).astype(
                jnp.bfloat16
            )
        )
        key_acc = key_acc + jnp.einsum(
            "hqk,qhd->khd", dscore, query_blk, preferred_element_type=jnp.float32
        )
    value_grad = value_acc.astype(jnp.bfloat16)
    query_grad = jnp.concatenate(query_parts, axis=0)
    key_grad = key_acc.astype(jnp.bfloat16)
    stacked = jnp.stack([query_grad, key_grad, value_grad], axis=1).reshape(seq_len, 3 * head_cols)
    summed = lax.psum_scatter(
        lax.dot_general(
            normed_all, stacked, (((0,), (0,)), ((), ())), preferred_element_type=jnp.float32
        ).astype(jnp.bfloat16),
        "dp",
        scatter_dimension=0,
        tiled=True,
    )
    return summed.reshape(shard_rows, 3, head_cols)


def solution(mesh):
    placed = (
        P(("dp", "tensor"), None),
        P(),
        P("dp", None, "tensor"),
        P(("dp", "tensor"), None),
        P(("dp", "tensor"), None),
        P("dp"),
    )
    return jax.shard_map(
        local, mesh=mesh, in_specs=placed, out_specs=P("dp", None, "tensor"), check_vma=False
    )
```

profile of v0, /device:TPU:6, one launch (start us, length us, event | category | flops | bytes accessed | tf_op | source)
XLA Modules:
  0.0 722.4 jit_solution(11057533517141475281)
XLA Ops:
  6.5 0.0 copy-start
  6.5 0.0 copy-start.3
  6.5 0.0 copy-start.2
  6.5 0.0 all-gather.5.cloned.1.call-start
  6.5 0.7 all-gather.5.cloned.1.call-update
  7.3 0.0 all-gather.3.cloned.1.call-start
  7.3 1.3 fusion.8
  8.6 2.1 fusion.10
  10.7 0.0 all-gather.3.cloned.1.call-update
  10.7 0.0 copy-done
  10.7 0.8 copy_bitcast_fusion.1
  11.5 18.0 %all-to-all-start = ((bf16[64,16,128]{2,0,1:T(8,128)(2,1)}), bf16[64,16,128]{2,0,1:T(8,128)(2,1)S(1)}, u32[]{:S(2)}, u32[]{:S(2)}) async-start(bf16[64,16,128]{2,0,1:T(8,128)(2,1)} %copy_bitcast_fusion.1), calls=%async_computation | async-start | bytes 524288 | tf_op jit(solution)/shard_map/all_to_all | solution.py:31
  29.6 0.0 copy-done.3
  29.6 0.0 copy-done.2
  29.6 0.8 copy_bitcast_fusion
  30.4 18.0 %all-to-all-done = bf16[64,16,128]{2,0,1:T(8,128)(2,1)S(1)} async-done(((bf16[64,16,128]{2,0,1:T(8,128)(2,1)}), bf16[64,16,128]{2,0,1:T(8,128)(2,1)S(1)}, u32[]{:S(2)}, u32[]{:S(2)}) %all-to-all-start) | async-done | bytes 262176 | tf_op jit(solution)/shard_map/all_to_all | solution.py:31
  48.4 6.3 all-to-all-start.1
  54.7 0.0 reduce-scatter.2.cloned.1.call-start
  54.8 197.1 %all-gather.5.cloned.1.call-done = bf16[4608,2,128]{2,1,0:T(2,128)(2,1)} async-done(((bf16[144,2,128]{2,1,0:T(2,128)(2,1)}), bf16[4608,2,128]{2,1,0:T(2,128)(2,1)}) %all-gather.5.cloned.1.call-update) | async-done | bytes 2359312 | tf_op jit(solution)/shard_map/all_gather | solution.py:24
  251.9 179.6 %all-gather.3.cloned.1.call-done = bf16[1024,4608]{1,0:T(8,128)(2,1)} async-done(((bf16[64,4608]{1,0:T(8,128)(2,1)}), bf16[1024,4608]{1,0:T(8,128)(2,1)}) %all-gather.3.cloned.1.call-update) | async-done | bytes 9437200 | tf_op jit(solution)/shard_map/all_gather | solution.py:22
  431.4 6.9 fusion.3
  438.4 0.4 fusion.26
  438.8 2.2 fusion.18
  441.0 0.0 all-to-all-done.1
  441.0 3.2 multiply_reduce_fusion
  444.2 1.0 fusion.20
  445.2 0.0 copy-start.1
  445.2 1.1 multiply_reduce_fusion.1
  446.3 0.5 copy-done.1
  446.8 2.7 multiply_convert_fusion
  449.5 0.5 fusion.13
  450.0 0.0 slice-start
  450.0 0.3 fusion.30
  450.3 0.0 slice-start.1
  450.3 0.0 slice-start.2
  450.3 1.0 fusion.11
  451.3 0.5 fusion.14
  451.8 0.3 fusion.12
  452.2 0.1 pad_maximum_fusion
  452.3 0.0 slice-done
  452.3 1.2 slice-done.1
  453.5 0.2 slice-done.2
  453.7 6.6 convolution_convert_fusion
  460.4 0.0 reduce-scatter.2.cloned.1.call-update
  460.4 253.9 %reduce-scatter.2.cloned.1.call-done = bf16[144,384]{1,0:T(8,128)(2,1)} async-done(((bf16[4608,384]{1,0:T(8,128)(2,1)}), bf16[144,384]{1,0:T(8,128)(2,1)}) %reduce-scatter.2.cloned.1.call-update) | async-done | bytes 110608 | tf_op jit(solution)/shard_map/reduce_scatter | solution.py:77
  714.3 1.6 copy_bitcast_fusion.2
  (6 shorter events, 0.1 us)
Async XLA Ops:
  6.5 4.2 copy-start
  6.5 23.0 %copy-start.3 = (s32[1024]{0:T(1024)S(1)}, s32[1024]{0:T(1024)}, u32[]{:S(2)}) copy-start(s32[1024]{0:T(1024)} %param.11) | copy-start | bytes 12292
  6.5 23.1 %copy-start.2 = (bf16[64,2048]{1,0:T(8,128)(2,1)S(1)}, bf16[64,2048]{1,0:T(8,128)(2,1)}, u32[]{:S(2)}) copy-start(bf16[64,2048]{1,0:T(8,128)(2,1)} %param.9) | copy-start | bytes 786436
  6.5 245.3 %all-gather.5.cloned.1.call-start = ((), (), s32[]{:S(2)}) async-start(), calls=%async_computation.4 | async-start | bytes 2433024 | tf_op jit(solution)/shard_map/all_gather | solution.py:24
  7.3 424.2 %all-gather.3.cloned.1.call-start = ((), (), s32[]{:S(2)}) async-start(), calls=%async_computation.3 | async-start | bytes 10027008 | tf_op jit(solution)/shard_map/all_gather | solution.py:22
  11.5 36.9 %all-to-all-start = ((bf16[64,16,128]{2,0,1:T(8,128)(2,1)}), bf16[64,16,128]{2,0,1:T(8,128)(2,1)S(1)}, u32[]{:S(2)}, u32[]{:S(2)}) async-start(bf16[64,16,128]{2,0,1:T(8,128)(2,1)} %copy_bitcast_fusion.1), calls=%async_computation | async-start | bytes 524288 | tf_op jit(solution)/shard_map/all_to_all | solution.py:31
  48.4 392.6 %all-to-all-start.1 = ((bf16[64,16,128]{2,0,1:T(8,128)(2,1)}), bf16[64,16,128]{2,0,1:T(8,128)(2,1)S(1)}, u32[]{:S(2)}, u32[]{:S(2)}) async-start(bf16[64,16,128]{2,0,1:T(8,128)(2,1)} %copy_bitcast_fusion), calls=%async_computation.1 | async-start | bytes 524288 | tf_op jit(solution)/shard_map/all_to_all | solution.py:32
  54.7 659.6 %reduce-scatter.2.cloned.1.call-start = ((), (), s32[]{:S(2)}) async-start(), calls=%async_computation.5 | async-start | bytes 3649536 | tf_op jit(solution)/shard_map/reduce_scatter | solution.py:77
  445.2 1.6 copy-start.1
  450.0 2.3 slice-start
  450.3 3.2 slice-start.1
  450.3 3.4 slice-start.2
Sparse Core Ops, SparseCore 0:
  9.4 242.3 all-gather.4
  255.2 176.2 all-gather.2
  460.5 253.7 reduce-scatter.1
where the time goes:
time: 723 us; the launch traced here: 722 us
  waiting for transfers between devices  649 us (90%)
  starting transfers between devices  24.4 us (3%)
  matrix products  24.1 us (3%)
  between operations  13.3 us (2%)
    reduce_scatter x1, waiting for transfers between devices, local(): lax.psum_scatter(lax.dot_general(normed_all, stacked, (((0,), (0,)), ((),...  254 us
    all_gather x1, waiting for transfers between devices, local(): lax.all_gather(qk_weight, 'dp', axis=0, tiled=True)  197 us
    all_gather x1, waiting for transfers between devices, local(): normed_all = lax.all_gather(normed, 'tensor', axis=0, tiled=True)  180 us
    all_to_all x1, starting transfers between devices, local(): lax.all_to_all(context_grad, 'tensor', split_axis=1, concat_axis=0, tiled...  18 us
    all_to_all x1, waiting for transfers between devices, local(): lax.all_to_all(context_grad, 'tensor', split_axis=1, concat_axis=0, tiled...  18 us
  transfers between devices with their start and end apart: 5, of which 4 were waited for; matrix products, arithmetic and copies ran while one was open for 2% of the time, Pallas kernels for 0%

commit v1 on v0

v1 whole, which is shorter than its diff:
```python
import functools

import jax
import jax.numpy as jnp
from jax import lax
from jax.experimental import pallas as pl
from jax.experimental.pallas import tpu as pltpu
from jax.sharding import PartitionSpec as P

MESH = pl.DeviceIdType.MESH
HD = 128
epsilon = 1e-06
softcap = 50.0
query_scale = 144.0 ** (-0.5)
NX, NY, NL = 4, 4, 8
SEQ = 1024
D = 4608
BLK = 144
QR = 16
NQ = 4
VMEM = pl.BlockSpec(memory_space=pltpu.VMEM)


def where_am_i():
    dp, t = lax.axis_index("dp"), lax.axis_index("tensor")
    return dp // NL, dp % NL, t // 8, (t // 2) % NX, t % 2


def device(y, zl, zh, x, c):
    return (y * NL + zl, zh * 8 + x * 2 + c)


def signal(target):
    pl.semaphore_signal(
        pltpu.get_barrier_semaphore(), inc=1, device_id=target, device_id_type=MESH
    )


class Sems:
    def __init__(self):
        self.at = {}
        self.n = 0

    def block(self, name, count):
        self.at[name] = self.n
        self.n += count


K1 = Sems()
for name, count in (
    ("L", 8), ("R", 8), ("O", 8), ("C", 32), ("Z", 4),
    ("WR", 8), ("WL", 8), ("YL", 8), ("YR", 8), ("YO", 8), ("AC", 16), ("AV", 16),
):
    K1.block(name, count)


def gather_kernel(
    tok, gain, w, ctx, val, nrm, proj, ctxo, valo, w_all, ssem, rsem
):
    y, zl, zh, x, c = where_am_i()
    me = zh * 8 + x * 2 + c
    left, right = (x + NX - 1) % NX, (x + 1) % NX
    opp = (x + 2) % NX
    to_left, to_right = device(y, zl, zh, left, c), device(y, zl, zh, right, c)
    to_core = device(y, zl, zh, x, 1 - c)
    to_far = device(y, zl, 1 - zh, x, c)
    y_lo, y_hi, y_op = (y + NY - 1) % NY, (y + 1) % NY, (y + 2) % NY
    to_ylo, to_yhi = device(y_lo, zl, zh, x, c), device(y_hi, zl, zh, x, c)
    has_lo, has_hi = zl > 0, zl < NL - 1
    to_zlo, to_zhi = device(y, zl - 1, zh, x, c), device(y, zl + 1, zh, x, c)

    def peer(d):
        t = (me + d) % 16
        return (y * NL + zl, t)

    for d in range(1, 16):
        signal(peer(d))
    signal(to_ylo)
    signal(to_yhi)

    @pl.when(has_lo)
    def _():
        signal(to_zlo)

    @pl.when(has_hi)
    def _():
        signal(to_zhi)

    own = me * 64
    for q in range(NQ):
        t = tok[q * QR : (q + 1) * QR, :].astype(jnp.float32)
        mean_sq = jnp.mean(t * t, axis=1, keepdims=True)
        n = (t * lax.rsqrt(mean_sq + epsilon) * gain[...]).astype(jnp.bfloat16)
        nrm[pl.ds(pl.multiple_of(own + q * QR, QR), QR), :] = n
    w_all[pl.ds(pl.multiple_of((y * NL + zl) * BLK, 16), BLK), :] = w[...]

    ends = (zl == 0).astype(jnp.int32) + (zl == NL - 1).astype(jnp.int32)
    pl.semaphore_wait(pltpu.get_barrier_semaphore(), 19 - ends)

    sent = []
    used = [0]

    def send(src, dst, r, target, cond=None):
        s = used[0]
        used[0] += 1
        copy = pltpu.make_async_remote_copy(
            src_ref=src, dst_ref=dst, send_sem=ssem.at[s], recv_sem=rsem.at[r],
            device_id=target, device_id_type=MESH,
        )
        copy.start()
        sent.append(copy)

    def got(ref, r):
        pltpu.make_async_remote_copy(
            src_ref=ref, dst_ref=ref, send_sem=ssem.at[0], recv_sem=rsem.at[r],
            device_id=to_core, device_id_type=MESH,
        ).wait_recv()

    def rows(h, xx, cc, q):
        r = h * 512 + xx * 128 + cc * 64 + q * QR
        return nrm.at[pl.ds(pl.multiple_of(r, QR), QR), :]

    def wrows(yy, b):
        return w_all.at[pl.ds(pl.multiple_of((yy * NL + b) * BLK, 16), BLK), :]

    def to_sister(k, h, xx, q):
        send(rows(h, xx, c, q), rows(h, xx, c, q), K1.at["C"] + k * 16 + xx * 4 + q, to_core)

    def spread(k, h, q):
        mine = rows(h, x, c, q)
        send(mine, mine, K1.at["L"] + k * 4 + q, to_right)
        send(mine, mine, K1.at["R"] + k * 4 + q, to_left)
        to_sister(k, h, x, q)

    def relay(k, h, q):
        from_left, from_right = rows(h, left, c, q), rows(h, right, c, q)
        got(from_left, K1.at["L"] + k * 4 + q)
        if q % 2 == 0:
            send(from_left, from_left, K1.at["O"] + k * 4 + q, to_right)
        to_sister(k, h, left, q)
        got(from_right, K1.at["R"] + k * 4 + q)
        if q % 2 == 1:
            send(from_right, from_right, K1.at["O"] + k * 4 + q, to_left)
        to_sister(k, h, right, q)

    def last(k, h, q):
        got(rows(h, opp, c, q), K1.at["O"] + k * 4 + q)
        to_sister(k, h, opp, q)

    far = 1 - zh
    for q in range(NQ):
        send(rows(zh, x, c, q), rows(zh, x, c, q), K1.at["Z"] + q, to_far)

    line = []
    s_line = used[0]
    used[0] += 16

    def along(cond, src, s, r, target):
        def copy():
            return pltpu.make_async_remote_copy(
                src_ref=src, dst_ref=src, send_sem=ssem.at[s_line + s],
                recv_sem=rsem.at[r], device_id=target, device_id_type=MESH,
            )

        @pl.when(cond)
        def _():
            copy().start()

        line.append((cond, copy))

    along(has_hi, wrows(y, zl), 0, K1.at["WR"] + 1, to_zhi)
    along(has_lo, wrows(y, zl), 8, K1.at["WL"] + 1, to_zlo)

    for q in range(NQ):
        spread(0, zh, q)

    s_y = used[0]
    used[0] += 16

    def y_copies(b):
        ref = wrows(y, b)
        return (
            pltpu.make_async_remote_copy(
                src_ref=ref, dst_ref=ref, send_sem=ssem.at[s_y + b],
                recv_sem=rsem.at[K1.at["YL"] + b], device_id=to_yhi, device_id_type=MESH,
            ),
            pltpu.make_async_remote_copy(
                src_ref=ref, dst_ref=ref, send_sem=ssem.at[s_y + 8 + b],
                recv_sem=rsem.at[K1.at["YR"] + b], device_id=to_ylo, device_id_type=MESH,
            ),
        )

    def y_spread(b):
        for copy in y_copies(b):
            copy.start()

    y_spread(zl)

    for d in range(1, 16):
        t = (me + d) % 16
        cols = pl.ds(pl.multiple_of(t * HD, HD), HD)
        here = pl.ds(pl.multiple_of(me * 64, 64), 64)
        send(ctx.at[:, cols], ctxo.at[here, :], K1.at["AC"] + d, peer(d))
        send(val.at[:, cols], valo.at[here, :], K1.at["AV"] + d, peer(d))
    here = pl.ds(pl.multiple_of(me * 64, 64), 64)
    mycols = pl.ds(pl.multiple_of(me * HD, HD), HD)
    ctxo[here, :] = ctx[:, mycols]
    valo[here, :] = val[:, mycols]

    def line_step(t):
        lo_ok, hi_ok = zl - t >= 0, zl + t <= NL - 1
        b_lo, b_hi = jnp.maximum(zl - t, 0), jnp.minimum(zl + t, NL - 1)

        @pl.when(lo_ok)
        def _():
            got(wrows(y, b_lo), K1.at["WR"] + t)

        if t < NL - 1:
            along(lo_ok & has_hi, wrows(y, b_lo), t, K1.at["WR"] + t + 1, to_zhi)

        @pl.when(lo_ok)
        def _():
            y_spread(b_lo)

        @pl.when(hi_ok)
        def _():
            got(wrows(y, b_hi), K1.at["WL"] + t)

        if t < NL - 1:
            along(hi_ok & has_lo, wrows(y, b_hi), 8 + t, K1.at["WL"] + t + 1, to_zlo)

        @pl.when(hi_ok)
        def _():
            y_spread(b_hi)

    line_step(1)
    relay(0, zh, 0)
    line_step(2)
    relay(0, zh, 1)
    last(0, zh, 0)
    line_step(3)
    relay(0, zh, 2)
    last(0, zh, 1)
    line_step(4)
    relay(0, zh, 3)
    last(0, zh, 2)
    line_step(5)
    last(0, zh, 3)
    line_step(6)
    line_step(7)
    for b in range(NL):
        lo, hi = wrows(y_lo, b), wrows(y_hi, b)
        got(lo, K1.at["YL"] + b)
        if b % 2 == 0:
            send(lo, lo, K1.at["YO"] + b, to_yhi)
        got(hi, K1.at["YR"] + b)
        if b % 2 == 1:
            send(hi, hi, K1.at["YO"] + b, to_ylo)
    for b in range(NL):
        got(wrows(y_op, b), K1.at["YO"] + b)

    def sister(k, h):
        for xx in range(NX):
            for q in range(NQ):
                got(rows(h, xx, 1 - c, q), K1.at["C"] + k * 16 + xx * 4 + q)

    def project(h):
        for r in range(2):
            part = pl.ds(pl.multiple_of(h * 512 + r * 256, 256), 256)
            proj[part, :] = jnp.dot(
                nrm[part, :], w_all[...], preferred_element_type=jnp.float32
            ).astype(jnp.bfloat16)

    sister(0, zh)
    project(zh)
    for q in range(NQ):
        got(rows(far, x, c, q), K1.at["Z"] + q)
        spread(1, far, q)
        if q > 0:
            relay(1, far, q - 1)
        if q > 1:
            last(1, far, q - 2)
    relay(1, far, NQ - 1)
    last(1, far, NQ - 2)
    last(1, far, NQ - 1)
    sister(1, far)
    project(far)
    for d in range(1, 16):
        t = (me + 16 - d) % 16
        there = pl.ds(pl.multiple_of(t * 64, 64), 64)
        got(ctxo.at[there, :], K1.at["AC"] + d)
        got(valo.at[there, :], K1.at["AV"] + d)
    for copy in sent:
        copy.wait_send()
    for cond, copy in line:

        @pl.when(cond)
        def _(copy=copy):
            copy().wait_send()

    for b in range(NL):
        for copy in y_copies(b):
            copy.wait_send()


N_SEND1 = 4 + 16 + 16 + 12 + 12 + 30 + 2 * (8 + 4 + 4) + 8 + 16


def attention_kernel(proj, ctx, val, start, out, dk_acc, dv_acc):
    qb = 256
    f32 = jnp.float32
    dk_acc[...] = jnp.zeros_like(dk_acc)
    dv_acc[...] = jnp.zeros_like(dv_acc)
    nt = (((1,), (1,)), ((), ()))
    tn = (((0,), (0,)), ((), ()))
    for i in range(SEQ // qb):
        lo, nk = i * qb, (i + 1) * qb
        q = proj[lo:nk, 0:HD]
        k = proj[0:nk, HD : 2 * HD]
        cot = ctx[lo:nk, :]
        raw = lax.dot_general(q, k, nt, preferred_element_type=f32)
        t = jnp.tanh(raw * (query_scale / softcap))
        keys = lax.broadcasted_iota(jnp.int32, (qb, nk), 1)
        pos = lo + lax.broadcasted_iota(jnp.int32, (qb, nk), 0)
        seen = (keys >= start[lo:nk, :]) & (keys <= pos)
        raised = jnp.where(seen, jnp.exp(t * softcap), 0.0)
        probs = raised * (1.0 / jnp.sum(raised, axis=1, keepdims=True))
        low = probs.astype(jnp.bfloat16)
        dv_acc[0:nk, :] += lax.dot_general(low, cot, tn, preferred_element_type=f32)
        dprobs = lax.dot_general(cot, val[0:nk, :], nt, preferred_element_type=f32)
        inner = jnp.sum(probs * dprobs, axis=1, keepdims=True)
        ds = (probs * (dprobs - inner) * ((1.0 - t * t) * query_scale)).astype(jnp.bfloat16)
        out[lo:nk, 0:HD] = jnp.dot(ds, k, preferred_element_type=f32).astype(jnp.bfloat16)
        dk_acc[0:nk, :] += lax.dot_general(ds, q, tn, preferred_element_type=f32)
    out[:, HD : 2 * HD] = dk_acc[...].astype(jnp.bfloat16)
    out[:, 2 * HD :] = dv_acc[...].astype(jnp.bfloat16)


K3 = Sems()
for name, count in (
    ("FL", 8), ("FR", 8), ("OL", 8), ("OR", 8), ("ZR", 8), ("ZL", 8),
):
    K3.block(name, count)
ORDER = (7, 0, 6, 1, 5, 2, 4, 3)


def scatter_kernel(
    nrm, grads, out, part, f_l, f_r, o_l, o_r, z_r, z_l, stage, total, ssem, rsem
):
    y, zl, zh, x, c = where_am_i()
    y_lo, y_hi, y_op = (y + NY - 1) % NY, (y + 1) % NY, (y + 2) % NY
    to_ylo, to_yhi = device(y_lo, zl, zh, x, c), device(y_hi, zl, zh, x, c)
    has_lo, has_hi = zl > 0, zl < NL - 1
    to_zlo, to_zhi = device(y, zl - 1, zh, x, c), device(y, zl + 1, zh, x, c)
    signal(to_ylo)
    signal(to_yhi)

    @pl.when(has_lo)
    def _():
        signal(to_zlo)

    @pl.when(has_hi)
    def _():
        signal(to_zhi)

    f32, bf16 = jnp.float32, jnp.bfloat16
    wide = D // NY

    def compute(slot, yy):
        cols = pl.ds(pl.multiple_of(yy * wide, 128), wide)
        part[slot] = lax.dot_general(
            nrm[:, cols], grads[...], (((0,), (0,)), ((), ())), preferred_element_type=f32
        ).astype(bf16)

    compute(2, y_op)
    ends = (zl == 0).astype(jnp.int32) + (zl == NL - 1).astype(jnp.int32)
    pl.semaphore_wait(pltpu.get_barrier_semaphore(), 4 - ends)

    sent = []
    used = [0]

    def send(src, dst, r, target):
        s = used[0]
        used[0] += 1
        copy = pltpu.make_async_remote_copy(
            src_ref=src, dst_ref=dst, send_sem=ssem.at[s], recv_sem=rsem.at[r],
            device_id=target, device_id_type=MESH,
        )
        copy.start()
        sent.append(copy)

    def got(ref, r):
        pltpu.make_async_remote_copy(
            src_ref=ref, dst_ref=ref, send_sem=ssem.at[0], recv_sem=rsem.at[r],
            device_id=to_yhi, device_id_type=MESH,
        ).wait_recv()

    def rows(b):
        return slice(b * BLK, (b + 1) * BLK)

    for i, b in enumerate(ORDER):
        src = part.at[2, rows(b), :]
        if i % 2 == 0:
            send(src, f_l.at[rows(b), :], K3.at["FL"] + b, to_yhi)
        else:
            send(src, f_r.at[rows(b), :], K3.at["FR"] + b, to_ylo)
    compute(1, y_hi)
    compute(3, y_lo)
    for i, b in enumerate(ORDER):
        if i % 2 == 0:
            got(f_l.at[rows(b), :], K3.at["FL"] + b)
            part[1, rows(b), :] = (
                part[1, rows(b), :].astype(f32) + f_l[rows(b), :].astype(f32)
            ).astype(bf16)
        else:
            got(f_r.at[rows(b), :], K3.at["FR"] + b)
            part[3, rows(b), :] = (
                part[3, rows(b), :].astype(f32) + f_r[rows(b), :].astype(f32)
            ).astype(bf16)
        send(part.at[1, rows(b), :], o_l.at[rows(b), :], K3.at["OL"] + b, to_yhi)
        send(part.at[3, rows(b), :], o_r.at[rows(b), :], K3.at["OR"] + b, to_ylo)
    compute(0, y)
    for b in ORDER:
        got(o_l.at[rows(b), :], K3.at["OL"] + b)
        got(o_r.at[rows(b), :], K3.at["OR"] + b)
        total[rows(b), :] = (
            part[0, rows(b), :].astype(f32)
            + o_l[rows(b), :].astype(f32)
            + o_r[rows(b), :].astype(f32)
        )

    line = []
    s_line = used[0]
    used[0] += 16

    def at(b):
        return pl.ds(pl.multiple_of(b * BLK, 16), BLK)

    def pass_on(s, cond, b, first, inbox, box_name, stage, target, slot):
        def copy():
            return pltpu.make_async_remote_copy(
                src_ref=stage.at[at(b), :], dst_ref=inbox.at[at(b), :],
                send_sem=ssem.at[s_line + slot], recv_sem=rsem.at[K3.at[box_name] + b],
                device_id=target, device_id_type=MESH,
            )

        @pl.when(cond)
        def _():
            @pl.when(jnp.logical_not(first))
            def _():
                got(inbox.at[at(b), :], K3.at[box_name] + b)
                stage[at(b), :] = (
                    total[at(b), :] + inbox[at(b), :].astype(f32)
                ).astype(bf16)

            @pl.when(first)
            def _():
                stage[at(b), :] = total[at(b), :].astype(bf16)

            copy().start()

        line.append((cond, copy))

    for s in range(NL - 1):
        b = jnp.minimum(NL - 1 + zl - s, NL - 1)
        pass_on(s, s >= zl, b, zl == 0, z_r, "ZR", stage, to_zhi, s)
        b = jnp.maximum(s - (NL - 1) + zl, 0)
        pass_on(s, s >= NL - 1 - zl, b, zl == NL - 1, z_l, "ZL", stage, to_zlo, 8 + s)

    @pl.when(has_lo)
    def _():
        got(z_r.at[at(zl), :], K3.at["ZR"] + zl)
        total[at(zl), :] += z_r[at(zl), :].astype(f32)

    @pl.when(has_hi)
    def _():
        got(z_l.at[at(zl), :], K3.at["ZL"] + zl)
        total[at(zl), :] += z_l[at(zl), :].astype(f32)

    out[...] = total[at(zl), :].astype(bf16)
    for copy in sent:
        copy.wait_send()
    for cond, copy in line:

        @pl.when(cond)
        def _(copy=copy):
            copy().wait_send()


N_SEND3 = 8 + 16 + 16


def local(tokens, gain, qk_weight, value_rows, context_grad, first_key):
    sds = jax.ShapeDtypeStruct
    bf16 = jnp.bfloat16
    w = qk_weight.reshape(BLK, 2 * HD)
    nrm, proj, ctx, val = pl.pallas_call(
        gather_kernel,
        out_shape=(
            sds((SEQ, D), bf16), sds((SEQ, 2 * HD), bf16),
            sds((SEQ, HD), bf16), sds((SEQ, HD), bf16),
        ),
        in_specs=[VMEM] * 5,
        out_specs=(VMEM,) * 4,
        scratch_shapes=[
            pltpu.VMEM((D, 2 * HD), bf16),
            pltpu.SemaphoreType.DMA((N_SEND1,)),
            pltpu.SemaphoreType.DMA((K1.n,)),
        ],
        compiler_params=pltpu.CompilerParams(
            collective_id=0, has_side_effects=True, vmem_limit_bytes=56 << 20
        ),
        name="gather",
    )(tokens, gain.reshape(1, D), w, context_grad, value_rows)
    start = (first_key - lax.axis_index("dp") * SEQ).reshape(SEQ, 1)
    grads = pl.pallas_call(
        attention_kernel,
        out_shape=sds((SEQ, 3 * HD), bf16),
        in_specs=[VMEM] * 4,
        out_specs=VMEM,
        scratch_shapes=[pltpu.VMEM((SEQ, HD), jnp.float32)] * 2,
        compiler_params=pltpu.CompilerParams(vmem_limit_bytes=56 << 20),
        name="attention",
    )(proj, ctx, val, start)
    wide = D // NY
    half = pltpu.VMEM((wide, 3 * HD), bf16)
    out = pl.pallas_call(
        scatter_kernel,
        out_shape=sds((BLK, 3 * HD), bf16),
        in_specs=[VMEM] * 2,
        out_specs=VMEM,
        scratch_shapes=[
            pltpu.VMEM((4, wide, 3 * HD), bf16),
            half, half, half, half, half, half, half,
            pltpu.VMEM((wide, 3 * HD), jnp.float32),
            pltpu.SemaphoreType.DMA((N_SEND3,)),
            pltpu.SemaphoreType.DMA((K3.n,)),
        ],
        compiler_params=pltpu.CompilerParams(
            collective_id=1, has_side_effects=True, vmem_limit_bytes=56 << 20
        ),
        name="scatter",
    )(nrm, grads)
    return out.reshape(BLK, 3, HD)


def solution(mesh):
    placed = (
        P(("dp", "tensor"), None),
        P(),
        P("dp", None, "tensor"),
        P(("dp", "tensor"), None),
        P(("dp", "tensor"), None),
        P("dp"),
    )
    return jax.shard_map(
        local, mesh=mesh, in_specs=placed, out_specs=P("dp", None, "tensor"), check_vma=False
    )
```

time: 723 us -> 237 us (0.33)
  waiting for transfers between devices: 649 us -> 0 us
  Pallas kernels: 0 us -> 229 us
  starting transfers between devices: 24.4 us -> 0 us
  matrix products: 24.1 us -> 0 us
  between operations: 13.3 us -> 0.02 us
    all_gather x2 -> x0, waiting for transfers between devices: 377 us -> none  [the longest x1 197 us: local(): lax.all_gather(qk_weight, 'dp', axis=0, tiled=True)]
    reduce_scatter x1 -> x0, waiting for transfers between devices: 254 us -> none  [local(): lax.psum_scatter(lax.dot_general(normed_all, stacked, (((0,), (0,)), ((),...]
    pallas_call x0 -> x3, Pallas kernels: none -> 229 us  [the longest x1 152 us: local(): pl.pallas_call(gather_kernel, out_shape=(sds((SEQ, D), bf16), sds((SEQ, 2...]
    all_to_all x2 -> x0, starting transfers between devices: 24.3 us -> none  [the longest x1 18 us: local(): lax.all_to_all(context_grad, 'tensor', split_axis=1, concat_axis=0, tiled...]
    dot_general x12 -> x0, matrix products: 24.1 us -> none  [the longest x1 6.95 us: local(): jnp.dot(normed_all, whole_w, preferred_element_type=jnp.float32)]
    all_to_all x2 -> x0, waiting for transfers between devices: 18 us -> none  [the longest x1 18 us: local(): lax.all_to_all(context_grad, 'tensor', split_axis=1, concat_axis=0, tiled...]
  transfers between devices with their start and end apart: 5 -> 0, of which waited for: 4 -> 0; matrix products, arithmetic and copies ran while one was open for 2% -> 0% of each run, Pallas kernels for 0% -> 0%
where the time goes in v1:
time: 237 us; the launch traced here: 235 us
  Pallas kernels  229 us (97%)
  local copies, waits for them, and re-layouts  5.45 us (2%)
    pallas_call x1, Pallas kernels, local(): pl.pallas_call(gather_kernel, out_shape=(sds((SEQ, D), bf16), sds((SEQ, 2...  152 us
    pallas_call x1, Pallas kernels, local(): pl.pallas_call(scatter_kernel, out_shape=sds((BLK, 3 * HD), bf16), in_spe...  70.5 us
    pallas_call x1, Pallas kernels, local(): pl.pallas_call(attention_kernel, out_shape=sds((SEQ, 3 * HD), bf16), in_s...  6.34 us

profile of v1, /device:TPU:6, one launch (start us, length us, event | category | flops | bytes accessed | tf_op | source)
XLA Modules:
  0.0 235.3 jit_solution(2620564499839281163)
XLA Ops:
  0.0 0.7 broadcast_subtract_fusion
  0.7 1.3 reshape.12.gain
  2.0 1.5 copy.14
  3.6 1.0 copy.8.start
  4.6 152.3 %gather.1 = (bf16[1024,4608]{1,0:T(8,128)(2,1)}, bf16[1024,256]{1,0:T(8,128)(2,1)}, bf16[1024,128]{1,0:T(8,128)(2,1)}, bf16[1024,128]{1,0:T(8,128)(2,1)}) custom-call(bf16[64,4608]{1,0:T(8,128)(2,1)} %tok.1, f32[1,4608]{1,0:T(1,128)} %reshape.12.gain, bf16[144,256]{1,0:T(8,128)(2,1)} %bitcast.10, bf16[64,2048]{1,0:T(8,128)(2,1)} %ctx.1, bf16[64,2048]{1,0:T(8,128)(2,1)} %val.1), custom_call_target="tpu_custom_call" | custom-call | tf_op jit(solution)/shard_map/gather/pallas_call | solution.py:497
  156.9 6.3 %attention.1.grads = bf16[1024,384]{1,0:T(8,128)(2,1)} custom-call(bf16[1024,256]{1,0:T(8,128)(2,1)} %get-tuple-element.10.proj, bf16[1024,128]{1,0:T(8,128)(2,1)} %get-tuple-element.11.ctx, bf16[1024,128]{1,0:T(8,128)(2,1)} %get-tuple-element.12.val, s32[1024,1]{1,0:T(8,128)} %copy.8.start), custom_call_target="tpu_custom_call" | custom-call | tf_op jit(solution)/shard_map/attention/pallas_call | solution.py:516
  163.2 70.5 %scatter.1 = bf16[144,384]{1,0:T(8,128)(2,1)} custom-call(bf16[1024,4608]{1,0:T(8,128)(2,1)} %get-tuple-element.9.nrm, bf16[1024,384]{1,0:T(8,128)(2,1)} %attention.1.grads), custom_call_target="tpu_custom_call" | custom-call | tf_op jit(solution)/shard_map/scatter/pallas_call | solution.py:527
  233.8 1.6 copy_bitcast_fusion

commit v2 on v0

v2 whole, which is shorter than its diff:
```python
import functools

import jax
import jax.numpy as jnp
from jax import lax
from jax.experimental import pallas as pl
from jax.experimental.pallas import tpu as pltpu
from jax.sharding import PartitionSpec as P

MESH = pl.DeviceIdType.MESH
HD = 128
epsilon = 1e-06
softcap = 50.0
query_scale = 144.0 ** (-0.5)
NX, NY, NL = 4, 4, 8
SEQ = 1024
D = 4608
BLK = 144
QR = 16
NQ = 4
VMEM = pl.BlockSpec(memory_space=pltpu.VMEM)


def where_am_i():
    dp, t = lax.axis_index("dp"), lax.axis_index("tensor")
    return dp // NL, dp % NL, t // 8, (t // 2) % NX, t % 2


def device(y, zl, zh, x, c):
    return (y * NL + zl, zh * 8 + x * 2 + c)


def signal(target):
    pl.semaphore_signal(
        pltpu.get_barrier_semaphore(), inc=1, device_id=target, device_id_type=MESH
    )


class Sems:
    def __init__(self):
        self.at = {}
        self.n = 0

    def block(self, name, count):
        self.at[name] = self.n
        self.n += count


SEM = Sems()
for name, count in (
    ("L", 8), ("R", 8), ("O", 8), ("C", 32), ("Z", 4), ("WR", 8), ("WL", 8),
    ("YL", 8), ("YR", 8), ("YO", 8), ("AC", 16), ("AV", 16),
    ("FL", 8), ("FR", 8), ("OL", 8), ("OR", 8), ("ZR", 8), ("ZL", 8),
):
    SEM.block(name, count)
N_SEND = 240
WIDE = D // NY


def attention(proj, ctx, val, start, out, dk_acc, dv_acc):
    qb = 256
    f32 = jnp.float32
    dk_acc[...] = jnp.zeros_like(dk_acc)
    dv_acc[...] = jnp.zeros_like(dv_acc)
    nt = (((1,), (1,)), ((), ()))
    tn = (((0,), (0,)), ((), ()))
    for i in range(SEQ // qb):
        lo, nk = i * qb, (i + 1) * qb
        q = proj[lo:nk, 0:HD]
        k = proj[0:nk, HD : 2 * HD]
        cot = ctx[lo:nk, :]
        raw = lax.dot_general(q, k, nt, preferred_element_type=f32)
        t = jnp.tanh(raw * (query_scale / softcap))
        keys = lax.broadcasted_iota(jnp.int32, (qb, nk), 1)
        pos = lo + lax.broadcasted_iota(jnp.int32, (qb, nk), 0)
        seen = (keys >= start[lo:nk, :]) & (keys <= pos)
        raised = jnp.where(seen, jnp.exp(t * softcap), 0.0)
        probs = raised * (1.0 / jnp.sum(raised, axis=1, keepdims=True))
        low = probs.astype(jnp.bfloat16)
        dv_acc[0:nk, :] += lax.dot_general(low, cot, tn, preferred_element_type=f32)
        dprobs = lax.dot_general(cot, val[0:nk, :], nt, preferred_element_type=f32)
        inner = jnp.sum(probs * dprobs, axis=1, keepdims=True)
        ds = (probs * (dprobs - inner) * ((1.0 - t * t) * query_scale)).astype(jnp.bfloat16)
        out[lo:nk, 0:HD] = jnp.dot(ds, k, preferred_element_type=f32).astype(jnp.bfloat16)
        dk_acc[0:nk, :] += lax.dot_general(ds, q, tn, preferred_element_type=f32)
    out[:, HD : 2 * HD] = dk_acc[...].astype(jnp.bfloat16)
    out[:, 2 * HD :] = dv_acc[...].astype(jnp.bfloat16)


def kernel(
    tok, gain, w, ctx, val, start, out,
    nrm, grads_t, w_all, proj, ctxo, valo, grads, dk_acc, dv_acc,
    part, f_l, f_r, o_l, o_r, z_r, z_l, stage, total, ssem, rsem,
):
    f32, bf16 = jnp.float32, jnp.bfloat16
    y, zl, zh, x, c = where_am_i()
    me = zh * 8 + x * 2 + c
    left, right = (x + NX - 1) % NX, (x + 1) % NX
    opp = (x + 2) % NX
    to_left, to_right = device(y, zl, zh, left, c), device(y, zl, zh, right, c)
    to_core = device(y, zl, zh, x, 1 - c)
    to_far = device(y, zl, 1 - zh, x, c)
    y_lo, y_hi, y_op = (y + NY - 1) % NY, (y + 1) % NY, (y + 2) % NY
    to_ylo, to_yhi = device(y_lo, zl, zh, x, c), device(y_hi, zl, zh, x, c)
    has_lo, has_hi = zl > 0, zl < NL - 1
    to_zlo, to_zhi = device(y, zl - 1, zh, x, c), device(y, zl + 1, zh, x, c)

    def peer(d):
        return (y * NL + zl, (me + d) % 16)

    for d in range(1, 16):
        signal(peer(d))

    @pl.when(has_lo)
    def _():
        signal(to_zlo)

    @pl.when(has_hi)
    def _():
        signal(to_zhi)

    signal(to_ylo)
    signal(to_yhi)

    own = me * 64
    for q in range(NQ):
        t = tok[q * QR : (q + 1) * QR, :].astype(f32)
        mean_sq = jnp.mean(t * t, axis=1, keepdims=True)
        n = (t * lax.rsqrt(mean_sq + epsilon) * gain[...]).astype(bf16)
        nrm[pl.ds(pl.multiple_of(own + q * QR, QR), QR), :] = n
    w_all[pl.ds(pl.multiple_of((y * NL + zl) * BLK, 16), BLK), :] = w[...]

    ends = (zl == 0).astype(jnp.int32) + (zl == NL - 1).astype(jnp.int32)
    pl.semaphore_wait(pltpu.get_barrier_semaphore(), 19 - ends)

    sent = []
    used = [0]

    def send(src, dst, r, target):
        s = used[0]
        used[0] += 1
        copy = pltpu.make_async_remote_copy(
            src_ref=src, dst_ref=dst, send_sem=ssem.at[s], recv_sem=rsem.at[r],
            device_id=target, device_id_type=MESH,
        )
        copy.start()
        sent.append(copy)

    def got(ref, r):
        pltpu.make_async_remote_copy(
            src_ref=ref, dst_ref=ref, send_sem=ssem.at[0], recv_sem=rsem.at[r],
            device_id=to_core, device_id_type=MESH,
        ).wait_recv()

    def rows(h, xx, cc, q):
        r = h * 512 + xx * 128 + cc * 64 + q * QR
        return nrm.at[pl.ds(pl.multiple_of(r, QR), QR), :]

    def wrows(yy, b):
        return w_all.at[pl.ds(pl.multiple_of((yy * NL + b) * BLK, 16), BLK), :]

    def to_sister(k, h, xx, q):
        send(rows(h, xx, c, q), rows(h, xx, c, q), SEM.at["C"] + k * 16 + xx * 4 + q, to_core)

    def spread(k, h, q):
        mine = rows(h, x, c, q)
        send(mine, mine, SEM.at["L"] + k * 4 + q, to_right)
        send(mine, mine, SEM.at["R"] + k * 4 + q, to_left)
        to_sister(k, h, x, q)

    def relay(k, h, q):
        from_left, from_right = rows(h, left, c, q), rows(h, right, c, q)
        got(from_left, SEM.at["L"] + k * 4 + q)
        if q % 2 == 0:
            send(from_left, from_left, SEM.at["O"] + k * 4 + q, to_right)
        to_sister(k, h, left, q)
        got(from_right, SEM.at["R"] + k * 4 + q)
        if q % 2 == 1:
            send(from_right, from_right, SEM.at["O"] + k * 4 + q, to_left)
        to_sister(k, h, right, q)

    def last(k, h, q):
        got(rows(h, opp, c, q), SEM.at["O"] + k * 4 + q)
        to_sister(k, h, opp, q)

    line = []

    def along(cond, src, slot, r, target):
        def copy():
            return pltpu.make_async_remote_copy(
                src_ref=src, dst_ref=src, send_sem=ssem.at[N_SEND - 32 + slot],
                recv_sem=rsem.at[r], device_id=target, device_id_type=MESH,
            )

        @pl.when(cond)
        def _():
            copy().start()

        line.append((cond, copy))

    def y_copies(b):
        ref = wrows(y, b)
        for k, to, box in ((0, to_yhi, "YL"), (1, to_ylo, "YR")):
            yield pltpu.make_async_remote_copy(
                src_ref=ref, dst_ref=ref, send_sem=ssem.at[N_SEND - 48 + 8 * k + b],
                recv_sem=rsem.at[SEM.at[box] + b], device_id=to, device_id_type=MESH,
            )

    def y_spread(b):
        for copy in y_copies(b):
            copy.start()

    def w_step(t):
        lo_ok, hi_ok = zl - t >= 0, zl + t <= NL - 1
        b_lo, b_hi = jnp.maximum(zl - t, 0), jnp.minimum(zl + t, NL - 1)

        @pl.when(lo_ok)
        def _():
            got(wrows(y, b_lo), SEM.at["WR"] + t)

        if t < NL - 1:
            along(lo_ok & has_hi, wrows(y, b_lo), t, SEM.at["WR"] + t + 1, to_zhi)

        @pl.when(hi_ok)
        def _():
            got(wrows(y, b_hi), SEM.at["WL"] + t)

        if t < NL - 1:
            along(hi_ok & has_lo, wrows(y, b_hi), 8 + t, SEM.at["WL"] + t + 1, to_zlo)

        @pl.when(lo_ok)
        def _():
            y_spread(b_lo)

        @pl.when(hi_ok)
        def _():
            y_spread(b_hi)

    def y_relay(b):
        lo, hi = wrows(y_lo, b), wrows(y_hi, b)
        got(lo, SEM.at["YL"] + b)
        if b % 2 == 0:
            send(lo, lo, SEM.at["YO"] + b, to_yhi)
        got(hi, SEM.at["YR"] + b)
        if b % 2 == 1:
            send(hi, hi, SEM.at["YO"] + b, to_ylo)

    far = 1 - zh
    along(has_hi, wrows(y, zl), 0, SEM.at["WR"] + 1, to_zhi)
    along(has_lo, wrows(y, zl), 8, SEM.at["WL"] + 1, to_zlo)
    for q in range(NQ):
        spread(0, zh, q)
    y_spread(zl)

    def to_other_half(q):
        send(rows(zh, x, c, q), rows(zh, x, c, q), SEM.at["Z"] + q, to_far)

    here = pl.ds(pl.multiple_of(me * 64, 64), 64)
    mycols = pl.ds(pl.multiple_of(me * HD, HD), HD)
    slot = x * 2 + c

    def heads_to(d, h, k):
        t = h * 8 + (slot + d) % 8
        cols = pl.ds(pl.multiple_of(t * HD, HD), HD)
        to = (y * NL + zl, t)
        send(ctx.at[:, cols], ctxo.at[here, :], SEM.at["AC"] + k * 8 + d, to)
        send(val.at[:, cols], valo.at[here, :], SEM.at["AV"] + k * 8 + d, to)

    def heads_from(d, h, k):
        there = pl.ds(pl.multiple_of((h * 8 + (slot + 8 - d) % 8) * 64, 64), 64)
        got(ctxo.at[there, :], SEM.at["AC"] + k * 8 + d)
        got(valo.at[there, :], SEM.at["AV"] + k * 8 + d)

    for d in range(1, 8):
        heads_to(d, zh, 0)
    ctxo[here, :] = ctx[:, mycols]
    valo[here, :] = val[:, mycols]

    def sister(k, h):
        for xx in range(NX):
            for q in range(NQ):
                got(rows(h, xx, 1 - c, q), SEM.at["C"] + k * 16 + xx * 4 + q)

    def project(h):
        for r in range(2):
            p = pl.ds(pl.multiple_of(h * 512 + r * 256, 256), 256)
            proj[p, :] = jnp.dot(nrm[p, :], w_all[...], preferred_element_type=f32).astype(bf16)

    def from_far(q):
        got(rows(far, x, c, q), SEM.at["Z"] + q)
        spread(1, far, q)
        if q < 2:
            to_other_half(q + 2)
        elif q == 2:
            for d in range(8):
                heads_to(d, far, 1)
        if q > 0:
            relay(1, far, q - 1)
        if q > 1:
            last(1, far, q - 2)

    w_step(1)
    relay(0, zh, 0)
    w_step(2)
    w_step(3)
    relay(0, zh, 1)
    last(0, zh, 0)
    w_step(4)
    w_step(5)
    relay(0, zh, 2)
    last(0, zh, 1)
    w_step(6)
    to_other_half(0)
    to_other_half(1)
    w_step(7)
    relay(0, zh, 3)
    last(0, zh, 2)
    last(0, zh, 3)
    for b in range(4):
        y_relay(b)
    from_far(0)
    for b in range(4, 8):
        y_relay(b)
    from_far(1)
    for b in range(NL):
        got(wrows(y_op, b), SEM.at["YO"] + b)
    sister(0, zh)
    project(zh)
    from_far(2)
    from_far(3)
    relay(1, far, NQ - 1)
    last(1, far, NQ - 2)
    last(1, far, NQ - 1)
    sister(1, far)
    project(far)
    for d in range(8):
        if d > 0:
            heads_from(d, zh, 0)
        heads_from(d, far, 1)

    attention(proj, ctxo, valo, start, grads, dk_acc, dv_acc)

    def unit(n):
        i = lax.broadcasted_iota(jnp.int32, (n, n), 0)
        j = lax.broadcasted_iota(jnp.int32, (n, n), 1)
        return jnp.where(i == j, 1.0, 0.0).astype(bf16)

    nt = (((1,), (1,)), ((), ()))
    grads_t[...] = lax.dot_general(
        unit(3 * HD), grads[...], nt, preferred_element_type=f32
    ).astype(bf16)

    def compute(slot, yy):
        for j in range(0, WIDE, 384):
            cols = pl.ds(pl.multiple_of(yy * WIDE + j, 128), 384)
            p = jnp.dot(grads_t[...], nrm[:, cols], preferred_element_type=f32).astype(bf16)
            part[slot, j : j + 384, :] = lax.dot_general(
                unit(384), p, nt, preferred_element_type=f32
            ).astype(bf16)

    def blk(b):
        return slice(b * BLK, (b + 1) * BLK)

    def at(b):
        return pl.ds(pl.multiple_of(b * BLK, 16), BLK)

    compute(2, y_op)
    for m in range(4):
        src = 7 - m
        send(part.at[2, blk(src), :], f_l.at[blk(src), :], SEM.at["FL"] + src, to_yhi)
        send(part.at[2, blk(m), :], f_r.at[blk(m), :], SEM.at["FR"] + m, to_ylo)
    compute(1, y_hi)
    compute(3, y_lo)
    for m in range(4):
        b = 7 - m
        got(f_l.at[blk(b), :], SEM.at["FL"] + b)
        part[1, blk(b), :] = (part[1, blk(b), :].astype(f32) + f_l[blk(b), :].astype(f32)).astype(bf16)
        send(part.at[1, blk(b), :], o_l.at[blk(b), :], SEM.at["OL"] + b, to_yhi)
        send(part.at[3, blk(b), :], o_r.at[blk(b), :], SEM.at["OR"] + b, to_ylo)
        got(f_r.at[blk(m), :], SEM.at["FR"] + m)
        part[3, blk(m), :] = (part[3, blk(m), :].astype(f32) + f_r[blk(m), :].astype(f32)).astype(bf16)
        send(part.at[1, blk(m), :], o_l.at[blk(m), :], SEM.at["OL"] + m, to_yhi)
        send(part.at[3, blk(m), :], o_r.at[blk(m), :], SEM.at["OR"] + m, to_ylo)
    compute(0, y)

    s_line = N_SEND - 16

    def pass_on(cond, b, first, inbox, box_name, target, slot):
        def copy():
            return pltpu.make_async_remote_copy(
                src_ref=stage.at[at(b), :], dst_ref=inbox.at[at(b), :],
                send_sem=ssem.at[s_line + slot], recv_sem=rsem.at[SEM.at[box_name] + b],
                device_id=target, device_id_type=MESH,
            )

        @pl.when(cond)
        def _():
            @pl.when(jnp.logical_not(first))
            def _():
                got(inbox.at[at(b), :], SEM.at[box_name] + b)
                stage[at(b), :] = (total[at(b), :] + inbox[at(b), :].astype(f32)).astype(bf16)

            @pl.when(first)
            def _():
                stage[at(b), :] = total[at(b), :].astype(bf16)

            copy().start()

        line.append((cond, copy))

    for s in range(NL - 1):
        if s < 4:
            for b in (7 - s, s):
                got(o_l.at[blk(b), :], SEM.at["OL"] + b)
                got(o_r.at[blk(b), :], SEM.at["OR"] + b)
                total[blk(b), :] = (
                    part[0, blk(b), :].astype(f32)
                    + o_l[blk(b), :].astype(f32)
                    + o_r[blk(b), :].astype(f32)
                )
        b = jnp.minimum(NL - 1 + zl - s, NL - 1)
        pass_on(s >= zl, b, zl == 0, z_r, "ZR", to_zhi, s)
        b = jnp.maximum(s - (NL - 1) + zl, 0)
        pass_on(s >= NL - 1 - zl, b, zl == NL - 1, z_l, "ZL", to_zlo, 8 + s)

    @pl.when(has_lo)
    def _():
        got(z_r.at[at(zl), :], SEM.at["ZR"] + zl)
        total[at(zl), :] += z_r[at(zl), :].astype(f32)

    @pl.when(has_hi)
    def _():
        got(z_l.at[at(zl), :], SEM.at["ZL"] + zl)
        total[at(zl), :] += z_l[at(zl), :].astype(f32)

    for j in range(3):
        out[j] = total[at(zl), j * HD : (j + 1) * HD].astype(bf16)
    assert used[0] <= N_SEND - 48
    for copy in sent:
        copy.wait_send()
    for b in range(NL):
        for copy in y_copies(b):
            copy.wait_send()
    for cond, copy in line:

        @pl.when(cond)
        def _(copy=copy):
            copy().wait_send()


def local(tokens, gain, qk_weight, value_rows, context_grad, first_key):
    f32, bf16 = jnp.float32, jnp.bfloat16
    start = (first_key - lax.axis_index("dp") * SEQ).reshape(SEQ, 1)
    wide = pltpu.VMEM((WIDE, 3 * HD), bf16)
    out = pl.pallas_call(
        kernel,
        out_shape=jax.ShapeDtypeStruct((3, BLK, HD), bf16),
        in_specs=[VMEM] * 6,
        out_specs=VMEM,
        scratch_shapes=[
            pltpu.VMEM((SEQ, D), bf16),
            pltpu.VMEM((3 * HD, SEQ), bf16),
            pltpu.VMEM((D, 2 * HD), bf16),
            pltpu.VMEM((SEQ, 2 * HD), bf16),
            pltpu.VMEM((SEQ, HD), bf16),
            pltpu.VMEM((SEQ, HD), bf16),
            pltpu.VMEM((SEQ, 3 * HD), bf16),
            pltpu.VMEM((SEQ, HD), f32),
            pltpu.VMEM((SEQ, HD), f32),
            pltpu.VMEM((4, WIDE, 3 * HD), bf16),
            wide, wide, wide, wide, wide, wide, wide,
            pltpu.VMEM((WIDE, 3 * HD), f32),
            pltpu.SemaphoreType.DMA((N_SEND,)),
            pltpu.SemaphoreType.DMA((SEM.n,)),
        ],
        compiler_params=pltpu.CompilerParams(
            collective_id=0, has_side_effects=True, vmem_limit_bytes=58 << 20
        ),
        name="layer",
    )(tokens, gain.reshape(1, D), qk_weight.reshape(BLK, 2 * HD), context_grad, value_rows, start)
    return jnp.transpose(out, (1, 0, 2))


def solution(mesh):
    placed = (
        P(("dp", "tensor"), None),
        P(),
        P("dp", None, "tensor"),
        P(("dp", "tensor"), None),
        P(("dp", "tensor"), None),
        P("dp"),
    )
    return jax.shard_map(
        local, mesh=mesh, in_specs=placed, out_specs=P("dp", None, "tensor"), check_vma=False
    )
```

time: 723 us -> 199 us (0.28)
  waiting for transfers between devices: 649 us -> 0 us
  Pallas kernels: 0 us -> 194 us
  starting transfers between devices: 24.4 us -> 0 us
  matrix products: 24.1 us -> 0 us
  between operations: 13.3 us -> 0.01 us
    all_gather x2 -> x0, waiting for transfers between devices: 377 us -> none  [the longest x1 197 us: local(): lax.all_gather(qk_weight, 'dp', axis=0, tiled=True)]
    reduce_scatter x1 -> x0, waiting for transfers between devices: 254 us -> none  [local(): lax.psum_scatter(lax.dot_general(normed_all, stacked, (((0,), (0,)), ((),...]
    pallas_call x0 -> x1, Pallas kernels: none -> 194 us  [local(): pl.pallas_call(kernel, out_shape=jax.ShapeDtypeStruct((3, BLK, HD), bf16)...]
    all_to_all x2 -> x0, starting transfers between devices: 24.3 us -> none  [the longest x1 18 us: local(): lax.all_to_all(context_grad, 'tensor', split_axis=1, concat_axis=0, tiled...]
    dot_general x12 -> x0, matrix products: 24.1 us -> none  [the longest x1 6.95 us: local(): jnp.dot(normed_all, whole_w, preferred_element_type=jnp.float32)]
    all_to_all x2 -> x0, waiting for transfers between devices: 18 us -> none  [the longest x1 18 us: local(): lax.all_to_all(context_grad, 'tensor', split_axis=1, concat_axis=0, tiled...]
  transfers between devices with their start and end apart: 5 -> 0, of which waited for: 4 -> 0; matrix products, arithmetic and copies ran while one was open for 2% -> 0% of each run, Pallas kernels for 0% -> 0%
where the time goes in v2:
time: 199 us
  Pallas kernels  194 us (97%)
  local copies, waits for them, and re-layouts  4.73 us (2%)
    pallas_call x1, Pallas kernels, local(): pl.pallas_call(kernel, out_shape=jax.ShapeDtypeStruct((3, BLK, HD), bf16)...  194 us

profile of v2, /device:TPU:6, one launch (start us, length us, event | category | flops | bytes accessed | tf_op | source)
XLA Modules:
  0.0 199.0 jit_solution(5605304747815600785)
XLA Ops:
  0.0 0.0 copy-start
  0.0 0.7 broadcast_subtract_fusion
  0.7 0.0 copy-done
  0.7 0.6 reshape.9.gain
  1.3 1.5 copy.10
  2.9 1.0 copy.7.start
  3.9 193.5 %layer.1 = bf16[3,144,128]{2,1,0:T(8,128)(2,1)} custom-call(bf16[64,4608]{1,0:T(8,128)(2,1)} %tok.1, f32[1,4608]{1,0:T(1,128)} %reshape.9.gain, bf16[144,256]{1,0:T(8,128)(2,1)} %bitcast.7, bf16[64,2048]{1,0:T(8,128)(2,1)} %ctx.1, bf16[64,2048]{1,0:T(8,128)(2,1)} %val.1, s32[1024,1]{1,0:T(8,128)} %copy.7.start), custom_call_target="tpu_custom_call" | custom-call | tf_op jit(solution)/shard_map/layer/pallas_call | solution.py:455
  197.4 1.5 copy.12
Async XLA Ops:
  0.0 0.7 copy-start

commit v3 on v2

--- a/solution.py
+++ b/solution.py
@@ -1,3 +1,5 @@
+import functools
+
 import functools
 
 import jax
@@ -50,46 +52,64 @@
 for name, count in (
     ("L", 8), ("R", 8), ("O", 8), ("C", 32), ("Z", 4), ("WR", 8), ("WL", 8),
     ("YL", 8), ("YR", 8), ("YO", 8), ("AC", 16), ("AV", 16),
-    ("FL", 8), ("FR", 8), ("OL", 8), ("OR", 8), ("ZR", 8), ("ZL", 8),
+    ("FL", 8), ("FR", 8), ("OL", 8), ("OR", 8), ("ZR", 24), ("ZL", 24),
 ):
     SEM.block(name, count)
 N_SEND = 240
 WIDE = D // NY
 
 
-def attention(proj, ctx, val, start, out, dk_acc, dv_acc):
-    qb = 256
-    f32 = jnp.float32
+QB = 256
+NT = (((1,), (1,)), ((), ()))
+TN = (((0,), (0,)), ((), ()))
+
+
+def softmax_part(proj, start, probs_t, slope_t):
+    for lo in range(0, SEQ, QB):
+        nk = lo + QB
+        raw = lax.dot_general(
+            proj[0:nk, HD : 2 * HD], proj[lo:nk, 0:HD], NT, preferred_element_type=jnp.float32
+        )
+        t = jnp.tanh(raw * (query_scale / softcap))
+        keys = lax.broadcasted_iota(jnp.int32, (nk, QB), 0)
+        pos = lo + lax.broadcasted_iota(jnp.int32, (nk, QB), 1)
+        seen = (keys >= start[:, lo:nk]) & (keys <= pos)
+        raised = jnp.where(seen, jnp.exp(t * softcap), 0.0)
+        probs_t[0:nk, lo:nk] = raised * (1.0 / jnp.sum(raised, axis=0, keepdims=True))
+        slope_t[0:nk, lo:nk] = (1.0 - t * t) * query_scale
+
+
+def gradient_part(proj, ctx, val, probs_t, slope_t, grads_t, dk_acc, dv_acc):
+    f32, bf16 = jnp.float32, jnp.bfloat16
     dk_acc[...] = jnp.zeros_like(dk_acc)
     dv_acc[...] = jnp.zeros_like(dv_acc)
-    nt = (((1,), (1,)), ((), ()))
-    tn = (((0,), (0,)), ((), ()))
-    for i in range(SEQ // qb):
-        lo, nk = i * qb, (i + 1) * qb
-        q = proj[lo:nk, 0:HD]
-        k = proj[0:nk, HD : 2 * HD]
+    for lo in range(0, SEQ, QB):
+        nk = lo + QB
         cot = ctx[lo:nk, :]
-        raw = lax.dot_general(q, k, nt, preferred_element_type=f32)
-        t = jnp.tanh(raw * (query_scale / softcap))
-        keys = lax.broadcasted_iota(jnp.int32, (qb, nk), 1)
-        pos = lo + lax.broadcasted_iota(jnp.int32, (qb, nk), 0)
-        seen = (keys >= start[lo:nk, :]) & (keys <= pos)
-        raised = jnp.where(seen, jnp.exp(t * softcap), 0.0)
-        probs = raised * (1.0 / jnp.sum(raised, axis=1, keepdims=True))
-        low = probs.astype(jnp.bfloat16)
-        dv_acc[0:nk, :] += lax.dot_general(low, cot, tn, preferred_element_type=f32)
-        dprobs = lax.dot_general(cot, val[0:nk, :], nt, preferred_element_type=f32)
-        inner = jnp.sum(probs * dprobs, axis=1, keepdims=True)
-        ds = (probs * (dprobs - inner) * ((1.0 - t * t) * query_scale)).astype(jnp.bfloat16)
-        out[lo:nk, 0:HD] = jnp.dot(ds, k, preferred_element_type=f32).astype(jnp.bfloat16)
-        dk_acc[0:nk, :] += lax.dot_general(ds, q, tn, preferred_element_type=f32)
-    out[:, HD : 2 * HD] = dk_acc[...].astype(jnp.bfloat16)
-    out[:, 2 * HD :] = dv_acc[...].astype(jnp.bfloat16)
+        probs = probs_t[0:nk, lo:nk]
+        dv_acc[0:nk, :] += jnp.dot(probs.astype(bf16), cot, preferred_element_type=f32)
+        dprobs = lax.dot_general(val[0:nk, :], cot, NT, preferred_element_type=f32)
+        inner = jnp.sum(probs * dprobs, axis=0, keepdims=True)
+        ds = (probs * (dprobs - inner) * slope_t[0:nk, lo:nk]).astype(bf16)
+        grads_t[0:HD, lo:nk] = lax.dot_general(
+            proj[0:nk, HD : 2 * HD], ds, TN, preferred_element_type=f32
+        ).astype(bf16)
+        dk_acc[0:nk, :] += jnp.dot(ds, proj[lo:nk, 0:HD], preferred_element_type=f32)
+    for k, acc in ((1, dk_acc), (2, dv_acc)):
+        grads_t[k * HD : (k + 1) * HD, :] = lax.dot_general(
+            unit(HD), acc[...].astype(bf16), NT, preferred_element_type=f32
+        ).astype(bf16)
+
+
+def unit(n):
+    i = lax.broadcasted_iota(jnp.int32, (n, n), 0)
+    j = lax.broadcasted_iota(jnp.int32, (n, n), 1)
+    return jnp.where(i == j, 1.0, 0.0).astype(jnp.bfloat16)
 
 
 def kernel(
     tok, gain, w, ctx, val, start, out,
-    nrm, grads_t, w_all, proj, ctxo, valo, grads, dk_acc, dv_acc,
+    nrm, grads_t, w_all, w_wide, proj, ctxo, valo, probs_t, slope_t, dk_acc, dv_acc,
     part, f_l, f_r, o_l, o_r, z_r, z_l, stage, total, ssem, rsem,
 ):
     f32, bf16 = jnp.float32, jnp.bfloat16
@@ -128,7 +148,11 @@
         mean_sq = jnp.mean(t * t, axis=1, keepdims=True)
         n = (t * lax.rsqrt(mean_sq + epsilon) * gain[...]).astype(bf16)
         nrm[pl.ds(pl.multiple_of(own + q * QR, QR), QR), :] = n
-    w_all[pl.ds(pl.multiple_of((y * NL + zl) * BLK, 16), BLK), :] = w[...]
+    w_wide[...] = w[...].astype(f32)
+    for j in range(2):
+        w_all[pl.ds(pl.multiple_of((y * NL + zl) * BLK, 16), BLK), j * HD : (j + 1) * HD] = w_wide[
+            pl.ds(j, BLK, stride=2), :
+        ].astype(bf16)
 
     ends = (zl == 0).astype(jnp.int32) + (zl == NL - 1).astype(jnp.int32)
     pl.semaphore_wait(pltpu.get_barrier_semaphore(), 19 - ends)
@@ -251,6 +275,7 @@
     for q in range(NQ):
         spread(0, zh, q)
     y_spread(zl)
+    send(rows(zh, x, c, 0), rows(zh, x, c, 0), SEM.at["Z"], to_far)
 
     def to_other_half(q):
         send(rows(zh, x, c, q), rows(zh, x, c, q), SEM.at["Z"] + q, to_far)
@@ -310,7 +335,6 @@
     relay(0, zh, 2)
     last(0, zh, 1)
     w_step(6)
-    to_other_half(0)
     to_other_half(1)
     w_step(7)
     relay(0, zh, 3)
@@ -333,29 +357,20 @@
     last(1, far, NQ - 1)
     sister(1, far)
     project(far)
+    softmax_part(proj, start, probs_t, slope_t)
     for d in range(8):
         if d > 0:
             heads_from(d, zh, 0)
         heads_from(d, far, 1)
 
-    attention(proj, ctxo, valo, start, grads, dk_acc, dv_acc)
-
-    def unit(n):
-        i = lax.broadcasted_iota(jnp.int32, (n, n), 0)
-        j = lax.broadcasted_iota(jnp.int32, (n, n), 1)
-        return jnp.where(i == j, 1.0, 0.0).astype(bf16)
-
-    nt = (((1,), (1,)), ((), ()))
-    grads_t[...] = lax.dot_general(
-        unit(3 * HD), grads[...], nt, preferred_element_type=f32
-    ).astype(bf16)
+    gradient_part(proj, ctxo, valo, probs_t, slope_t, grads_t, dk_acc, dv_acc)
 
     def compute(slot, yy):
         for j in range(0, WIDE, 384):
             cols = pl.ds(pl.multiple_of(yy * WIDE + j, 128), 384)
             p = jnp.dot(grads_t[...], nrm[:, cols], preferred_element_type=f32).astype(bf16)
             part[slot, j : j + 384, :] = lax.dot_general(
-                unit(384), p, nt, preferred_element_type=f32
+                unit(384), p, NT, preferred_element_type=f32
             ).astype(bf16)
 
     def blk(b):
@@ -383,58 +398,66 @@
         send(part.at[3, blk(m), :], o_r.at[blk(m), :], SEM.at["OR"] + m, to_ylo)
     compute(0, y)
 
-    s_line = N_SEND - 16
 
     def pass_on(cond, b, first, inbox, box_name, target, slot):
-        def copy():
+        def copy(j):
             return pltpu.make_async_remote_copy(
-                src_ref=stage.at[at(b), :], dst_ref=inbox.at[at(b), :],
-                send_sem=ssem.at[s_line + slot], recv_sem=rsem.at[SEM.at[box_name] + b],
+                src_ref=stage.at[j, at(b), :], dst_ref=inbox.at[j, at(b), :],
+                send_sem=ssem.at[N_SEND + slot * 3 + j],
+                recv_sem=rsem.at[SEM.at[box_name] + 8 * j + b],
                 device_id=target, device_id_type=MESH,
             )
 
         @pl.when(cond)
         def _():
-            @pl.when(jnp.logical_not(first))
-            def _():
-                got(inbox.at[at(b), :], SEM.at[box_name] + b)
-                stage[at(b), :] = (total[at(b), :] + inbox[at(b), :].astype(f32)).astype(bf16)
-
-            @pl.when(first)
-            def _():
-                stage[at(b), :] = total[at(b), :].astype(bf16)
-
-            copy().start()
-
-        line.append((cond, copy))
+            for j in range(3):
+
+                @pl.when(jnp.logical_not(first))
+                def _(j=j):
+                    got(inbox.at[j, at(b), :], SEM.at[box_name] + 8 * j + b)
+                    stage[j, at(b), :] = (
+                        total[j, at(b), :] + inbox[j, at(b), :].astype(f32)
+                    ).astype(bf16)
+
+                @pl.when(first)
+                def _(j=j):
+                    stage[j, at(b), :] = total[j, at(b), :].astype(bf16)
+
+                copy(j).start()
+
+        for j in range(3):
+            line.append((cond, functools.partial(copy, j)))
 
     for s in range(NL - 1):
         if s < 4:
             for b in (7 - s, s):
                 got(o_l.at[blk(b), :], SEM.at["OL"] + b)
                 got(o_r.at[blk(b), :], SEM.at["OR"] + b)
-                total[blk(b), :] = (
-                    part[0, blk(b), :].astype(f32)
-                    + o_l[blk(b), :].astype(f32)
-                    + o_r[blk(b), :].astype(f32)
-                )
+                for j in range(3):
+                    c3 = slice(j * HD, (j + 1) * HD)
+                    total[j, blk(b), :] = (
+                        part[0, blk(b), c3].astype(f32)
+                        + o_l[blk(b), c3].astype(f32)
+                        + o_r[blk(b), c3].astype(f32)
+                    )
         b = jnp.minimum(NL - 1 + zl - s, NL - 1)
         pass_on(s >= zl, b, zl == 0, z_r, "ZR", to_zhi, s)
         b = jnp.maximum(s - (NL - 1) + zl, 0)
         pass_on(s >= NL - 1 - zl, b, zl == NL - 1, z_l, "ZL", to_zlo, 8 + s)
 
-    @pl.when(has_lo)
-    def _():
-        got(z_r.at[at(zl), :], SEM.at["ZR"] + zl)
-        total[at(zl), :] += z_r[at(zl), :].astype(f32)
-
-    @pl.when(has_hi)
-    def _():
-        got(z_l.at[at(zl), :], SEM.at["ZL"] + zl)
-        total[at(zl), :] += z_l[at(zl), :].astype(f32)
-
     for j in range(3):
-        out[j] = total[at(zl), j * HD : (j + 1) * HD].astype(bf16)
+
+        @pl.when(has_lo)
+        def _(j=j):
+            got(z_r.at[j, at(zl), :], SEM.at["ZR"] + 8 * j + zl)
+            total[j, at(zl), :] += z_r[j, at(zl), :].astype(f32)
+
+        @pl.when(has_hi)
+        def _(j=j):
+            got(z_l.at[j, at(zl), :], SEM.at["ZL"] + 8 * j + zl)
+            total[j, at(zl), :] += z_l[j, at(zl), :].astype(f32)
+
+        out[j] = total[j, at(zl), :].astype(bf16)
     assert used[0] <= N_SEND - 48
     for copy in sent:
         copy.wait_send()
@@ -450,8 +473,8 @@
 
 def local(tokens, gain, qk_weight, value_rows, context_grad, first_key):
     f32, bf16 = jnp.float32, jnp.bfloat16
-    start = (first_key - lax.axis_index("dp") * SEQ).reshape(SEQ, 1)
-    wide = pltpu.VMEM((WIDE, 3 * HD), bf16)
+    start = (first_key - lax.axis_index("dp") * SEQ).reshape(1, SEQ)
+    wide, deep = pltpu.VMEM((WIDE, 3 * HD), bf16), pltpu.VMEM((3, WIDE, HD), bf16)
     out = pl.pallas_call(
         kernel,
         out_shape=jax.ShapeDtypeStruct((3, BLK, HD), bf16),
@@ -461,23 +484,25 @@
             pltpu.VMEM((SEQ, D), bf16),
             pltpu.VMEM((3 * HD, SEQ), bf16),
             pltpu.VMEM((D, 2 * HD), bf16),
+            pltpu.VMEM((2 * BLK, HD), f32),
             pltpu.VMEM((SEQ, 2 * HD), bf16),
             pltpu.VMEM((SEQ, HD), bf16),
             pltpu.VMEM((SEQ, HD), bf16),
-            pltpu.VMEM((SEQ, 3 * HD), bf16),
+            pltpu.VMEM((SEQ, SEQ), f32),
+            pltpu.VMEM((SEQ, SEQ), f32),
             pltpu.VMEM((SEQ, HD), f32),
             pltpu.VMEM((SEQ, HD), f32),
             pltpu.VMEM((4, WIDE, 3 * HD), bf16),
-            wide, wide, wide, wide, wide, wide, wide,
-            pltpu.VMEM((WIDE, 3 * HD), f32),
-            pltpu.SemaphoreType.DMA((N_SEND,)),
+            wide, wide, wide, wide, deep, deep, deep,
+            pltpu.VMEM((3, WIDE, HD), f32),
+            pltpu.SemaphoreType.DMA((N_SEND + 48,)),
             pltpu.SemaphoreType.DMA((SEM.n,)),
         ],
         compiler_params=pltpu.CompilerParams(
             collective_id=0, has_side_effects=True, vmem_limit_bytes=58 << 20
         ),
         name="layer",
-    )(tokens, gain.reshape(1, D), qk_weight.reshape(BLK, 2 * HD), context_grad, value_rows, start)
+    )(tokens, gain.reshape(1, D), qk_weight.reshape(2 * BLK, HD), context_grad, value_rows, start)
     return jnp.transpose(out, (1, 0, 2))
 
 

time: 199 us -> 186 us (0.935); the launches traced: 199 us -> 183 us
  Pallas kernels: 194 us -> 179 us
  local copies, waits for them, and re-layouts: 4.73 us -> 2.17 us
    pallas_call x1, Pallas kernels: 194 us -> 179 us  [local(): pl.pallas_call(kernel, out_shape=jax.ShapeDtypeStruct((3, BLK, HD), bf16)...]
where the time goes in v3:
time: 186 us; the launch traced here: 183 us
  Pallas kernels  179 us (96%)
  local copies, waits for them, and re-layouts  2.17 us (1%)
    pallas_call x1, Pallas kernels, local(): pl.pallas_call(kernel, out_shape=jax.ShapeDtypeStruct((3, BLK, HD), bf16)...  179 us

profile of v3, /device:TPU:6, one launch (start us, length us, event | category | flops | bytes accessed | tf_op | source)
XLA Modules:
  0.0 182.8 jit_solution(10877116431287738014)
XLA Ops:
  0.0 0.0 copy-start
  0.0 1.3 broadcast_subtract_fusion
  1.3 0.0 copy-done
  1.3 0.6 reshape.9.gain
  1.9 179.3 %layer.1 = bf16[3,144,128]{2,1,0:T(8,128)(2,1)} custom-call(bf16[64,4608]{1,0:T(8,128)(2,1)} %tok.1, f32[1,4608]{1,0:T(1,128)} %reshape.9.gain, bf16[288,128]{1,0:T(8,128)(2,1)} %bitcast.4, bf16[64,2048]{1,0:T(8,128)(2,1)} %ctx.1, bf16[64,2048]{1,0:T(8,128)(2,1)} %val.1, s32[1,1024]{1,0:T(1,128)} %bitcast.5), custom_call_target="tpu_custom_call" | custom-call | tf_op jit(solution)/shard_map/layer/pallas_call | solution.py:478
  181.2 1.5 copy.8
Async XLA Ops:
  0.0 1.3 copy-start

commit v4 on v3

--- a/solution.py
+++ b/solution.py
@@ -314,9 +314,7 @@
     def from_far(q):
         got(rows(far, x, c, q), SEM.at["Z"] + q)
         spread(1, far, q)
-        if q < 2:
-            to_other_half(q + 2)
-        elif q == 2:
+        if q == 1:
             for d in range(8):
                 heads_to(d, far, 1)
         if q > 0:
@@ -336,6 +334,8 @@
     last(0, zh, 1)
     w_step(6)
     to_other_half(1)
+    to_other_half(2)
+    to_other_half(3)
     w_step(7)
     relay(0, zh, 3)
     last(0, zh, 2)

time: 186 us -> 183 us (0.984)
  no operation moved by 1% of the time
where the time goes in v4:
time: 183 us; the launch traced here: 182 us
  Pallas kernels  178 us (97%)
  local copies, waits for them, and re-layouts  2.17 us (1%)
    pallas_call x1, Pallas kernels, local(): pl.pallas_call(kernel, out_shape=jax.ShapeDtypeStruct((3, BLK, HD), bf16)...  178 us

profile of v4, /device:TPU:6, one launch (start us, length us, event | category | flops | bytes accessed | tf_op | source)
XLA Modules:
  0.0 181.6 jit_solution(9892452782533901446)
XLA Ops:
  0.0 0.0 copy-start
  0.0 1.3 broadcast_subtract_fusion
  1.3 0.0 copy-done
  1.3 0.6 reshape.9.gain
  1.9 178.1 %layer.1 = bf16[3,144,128]{2,1,0:T(8,128)(2,1)} custom-call(bf16[64,4608]{1,0:T(8,128)(2,1)} %tok.1, f32[1,4608]{1,0:T(1,128)} %reshape.9.gain, bf16[288,128]{1,0:T(8,128)(2,1)} %bitcast.4, bf16[64,2048]{1,0:T(8,128)(2,1)} %ctx.1, bf16[64,2048]{1,0:T(8,128)(2,1)} %val.1, s32[1,1024]{1,0:T(1,128)} %bitcast.5), custom_call_target="tpu_custom_call" | custom-call | tf_op jit(solution)/shard_map/layer/pallas_call | solution.py:478
  180.1 1.5 copy.8
Async XLA Ops:
  0.0 1.3 copy-start
